TPU v7x, 32 devices: a whole 2x2x4 slice. The times are simulated.
32 devices in a mesh: district: 2 (over x), tile: 16 (over z, y, core).
Axes of the slice: x: 2, y: 2, z: 4, core: 2. Of those that a mesh axis runs over, the one named last changes fastest.
Arguments:
- cotangent: bfloat16 [384, 49152], P('tile', 'district'), parts along dimension 1, may hold values from -6 to 6
- coeffs: bfloat16 [2305, 49152], P(None, ('district', 'tile')), parts along dimension 1, may hold values from -0.0390625 to 0.0390625
- ctf: float32 [8, 24], replicated, may hold values from -1.5 to 1.5
- tap_count: int32 [8], replicated, may hold values from 1 to 24, as said below
- construction: int32 [49152], P('district'), parts along dimension 0, may hold values from 0 to 7
Outputs:
- sky_grad: float32 [384, 4610], P('tile', 'district'), parts along dimension 1
There are 2 independent parts, one for each index of `district`. A program takes and returns all parts, laid end to end along the dimension named above; an argument that names none is the same for every part. Nothing has to cross between parts.
Inputs may be any that keep to these rules, and one draw needn't show every extreme that they name: `tap_count`: some type has 24 live taps and some has one.
All inputs are finite; a program needn't handle non-finite values.
Results may differ from a plain program's by a relative error of at most 0.0029.
Values may be sent and summed in bfloat16 or wider, within the bound.
A program may use at most 128 MiB of HBM per device.

v0:
```python
import jax
import jax.numpy as jnp
from jax import lax
from jax.sharding import PartitionSpec as P


def shifted(value, axis, by):
    size = lax.axis_size(axis)
    pairs = [(i, i + by) for i in range(size) if 0 <= i + by < size]
    return lax.ppermute(value, axis, pairs)


def taps_table(kinds, tap_count, ctf):
    onehot = (kinds[:, None] == jnp.arange(ctf.shape[0], dtype=jnp.int32)[None, :]).astype(
        jnp.float32
    )
    live = jnp.where(
        jnp.arange(ctf.shape[1], dtype=jnp.int32)[None, :] < tap_count[:, None],
        ctf,
        jnp.float32(0.0),
    )
    return jnp.einsum("sc,ck->ks", onehot, live, precision=lax.Precision.HIGHEST)


def correlate(extended, taps, length):
    accum = jnp.zeros((length, extended.shape[1]), jnp.float32)
    for shift_k in range(taps.shape[0]):
        accum = accum + taps[shift_k][None, :] * extended[shift_k : shift_k + length].astype(
            jnp.float32
        )
    return accum.astype(jnp.bfloat16)


def per_device(cotangent, coeffs, ctf, tap_count, construction):
    span = ctf.shape[1]
    hours = cotangent.shape[0]
    taps = taps_table(construction, tap_count, ctf)
    tail = shifted(cotangent[: span - 1], "tile", -1)
    extended = jnp.concatenate([cotangent, tail], 0)
    surface = correlate(extended, taps, hours)
    by_points = lax.all_to_all(surface, "tile", split_axis=1, concat_axis=0, tiled=True)
    partial_value = lax.dot_general(
        by_points, coeffs, (((1,), (1,)), ((), ())), preferred_element_type=jnp.float32
    )
    return lax.psum_scatter(partial_value, "tile", scatter_dimension=0, tiled=True)


def solution(mesh):
    return jax.shard_map(
        per_device,
        mesh=mesh,
        in_specs=(P("tile", "district"), P(None, ("district", "tile")), P(), P(), P("district")),
        out_specs=P("tile", "district"),
        check_vma=False,
    )
```

profile of v0, /device:TPU:0, one launch (start us, length us, event | category | flops | bytes accessed | tf_op | source)
XLA Modules:
  0.0 148.4 jit_solution(18111956519017167114)
XLA Ops:
  6.5 0.0 reduce-scatter.4.cloned.1.call-start
  6.5 1.3 collective-permute-start
  7.8 2.1 %fusion = f32[24,24576]{1,0:T(8,128)S(1)} fusion(s32[24576]{0:T(1024)} %param.9, f32[8,24]{1,0:T(8,128)} %param.7, s32[8]{0:T(128)} %param.8), kind=kOutput, calls=%fused_computation.3 | convolution fusion | flops 56820096 | bytes 2458400 | tf_op jit(solution)/shard_map/sc,ck->ks/dot_general | solution.py:22
  9.9 0.0 copy-start
  10.0 1.6 %fusion.6 = (f32[1,24576]{1,0:T(1,128)S(1)}, f32[1,24576]{1,0:T(1,128)S(1)}, f32[1,24576]{1,0:T(1,128)S(1)}, f32[1,24576]{1,0:T(1,128)S(1)}, f32[1,24576]{1,0:T(...) fusion(f32[24,24576]{1,0:T(8,128)S(1)} %fusion), kind=kLoop, calls=%fused_computation.12 | loop fusion | bytes 3735552 | tf_op jit(solution)/shard_map/slice | solution.py:28
  11.6 0.4 fusion.7
  12.0 0.0 copy-done
  12.0 0.1 constant_dynamic-update-slice_fusion.1
  12.0 0.0 collective-permute-done
  12.1 0.0 slice-start
  12.1 0.1 constant_dynamic-update-slice_fusion
  12.2 0.0 slice-start.1
  12.2 7.4 %add_convert_fusion = bf16[24,24576]{1,0:T(8,128)(2,1)S(1)} fusion(bf16[24,24576]{1,0:T(8,128)(2,1)S(1)} %copy-done, bf16[47,24576]{1,0:T(8,128)(2,1)S(1)} %constant_dynamic-update-slice_fusion, f32[24576]{0:T(1024)S(1)} %bitcast.40, f32[24576]{0:T(1024)S(1)} %bitcast.41, f32[24576]{0:T(1024)S(1)} %bitcast.42, f32[24576]{0:T(1024)S(1)} %bitcast.43, ...), kind=kLoop, calls=%fused_computation | loop fusion | flops 42467328 | bytes 31850496 | tf_op jit(solution)/shard_map/convert_element_type | solution.py:31
  19.6 0.1 copy.11
  19.7 48.2 %all_to_all.19 = bf16[24,16,1536]{2,0,1:T(8,128)(2,1)S(1)} all-to-all(bf16[24,16,1536]{2,0,1:T(8,128)(2,1)S(1)} %bitcast.37), channel_id=1, replica_groups=mesh['district'=2,'tile'=16] {'tile'}, dimensions={1} | all-to-all | bytes 2359296 | tf_op jit(solution)/shard_map/all_to_all | solution.py:41
  67.9 0.0 slice-done
  67.9 0.0 slice-done.1
  67.9 5.1 %fusion.8 = f32[384,2305]{1,0:T(8,128)} fusion(bf16[384,1536]{1,0:T(8,128)(2,1)S(1)} %bitcast.38, bf16[2305,1536]{1,0:T(8,128)(2,1)S(1)} %bitcast.64), kind=kOutput, calls=%fused_computation.14 | convolution fusion | flops 2719088640 | bytes 11801088 | tf_op jit(solution)/shard_map/dot_general | solution.py:42
  72.9 0.0 reduce-scatter.4.cloned.1.call-update
  73.0 68.6 %reduce-scatter.4.cloned.1.call-done = f32[24,2305]{1,0:T(8,128)} async-done(((f32[384,2305]{1,0:T(8,128)}), f32[24,2305]{1,0:T(8,128)}) %reduce-scatter.4.cloned.1.call-update) | async-done | bytes 221296
  (1 shorter events, 0.0 us)
Async XLA Ops:
  6.5 135.0 %reduce-scatter.4.cloned.1.call-start = ((), (), s32[]{:S(2)}) async-start(), calls=%async_computation.2 | async-start | bytes 3969024
  6.5 5.5 %collective-permute-start = (bf16[23,24576]{1,0:T(8,128)(2,1)}, bf16[23,24576]{1,0:T(8,128)(2,1)S(1)}, u32[]{:S(2)}, u32[]{:S(2)}) collective-permute-start(bf16[23,24576]{1,0:T(8,128)(2,1)} %bitcast.35), channel_id=1, source_target_pairs={{1,0},{2,1},{3,2},{4,3},{5,4},{6,5},{7,6},{8,7},{9,8},{10,9},{11,1... | collective-permute-start | bytes 3391496 | tf_op jit(solution)/shard_map/ppermute | solution.py:10
  9.9 2.0 %copy-start = (bf16[24,24576]{1,0:T(8,128)(2,1)S(1)}, bf16[24,24576]{1,0:T(8,128)(2,1)}, u32[]{:S(2)}) copy-start(bf16[24,24576]{1,0:T(8,128)(2,1)} %param.5) | copy-start | bytes 3538948
  12.1 55.8 %slice-start = ((s8[7102464]{0:T(1024)(128)(4,1)}), s8[4194304]{0:T(1024)(128)(4,1)S(1)}, s32[]{:S(2)}) async-start(s8[7102464]{0:T(1024)(128)(4,1)} %bitcast.63), calls=%async_computation.3 | async-start | bytes 8388608
  12.2 55.7 %slice-start.1 = ((s8[7102464]{0:T(1024)(128)(4,1)}), s8[2908160]{0:T(1024)(128)(4,1)S(1)}, s32[]{:S(2)}) async-start(s8[7102464]{0:T(1024)(128)(4,1)} %bitcast.63), calls=%async_computation.4 | async-start | bytes 5816320
Sparse Core Ops, SparseCore 0:
  73.1 68.3 reduce-scatter.3
where the time goes:
time: 149 us; the launch traced here: 148 us
  waiting for transfers between devices  68.6 us (46%)
  blocking collectives  48.2 us (32%)
  between operations  13.5 us (9%)
  other arithmetic  7.44 us (5%)
  matrix products  7.16 us (5%)
  local copies, waits for them, and re-layouts  2.24 us (2%)
    unnamed x2, waiting for transfers between devices  68.6 us
    all_to_all x1, blocking collectives, per_device(): lax.all_to_all(surface, 'tile', split_axis=1, concat_axis=0, tiled=True)  48.2 us
    convert_element_type x1, other arithmetic, correlate(): return accum.astype(jnp.bfloat16)  7.44 us
    dot_general x1, matrix products, per_device(): lax.dot_general(by_points, coeffs, (((1,), (1,)), ((), ())), preferred_el...  5.05 us
  transfers between devices with their start and end apart: 2, of which 1 were waited for; matrix products, arithmetic and copies ran while one was open for 3% of the time, Pallas kernels for 0%

commit v1 on v0

v1 whole, which is shorter than its diff:
```python
import functools

import jax
import jax.numpy as jnp
from jax import lax
from jax.experimental import pallas as pl
from jax.experimental.pallas import tpu as pltpu
from jax.sharding import PartitionSpec as P

MESH = pl.DeviceIdType.MESH
LANES = 128
CHUNK = 256
PLANE = 4


def kernel(
    n, cot, coeffs, kinds_all, ctf, tap_count, out,
    recv, weights, kinds, taps, ext, surf, csend, crecv, keep, ysend, yrecv, ykeep, zsend, zrecv,
    a_send, a_recv, c_send, c_recv, y_send, y_recv, z_send, z_recv, local,
):
    hours = cot.shape[0]
    points = coeffs.shape[1]
    patches = coeffs.shape[0]
    span = ctf.shape[1]
    types = ctf.shape[0]
    groups = n // PLANE
    rows = PLANE * hours
    tiles = points // LANES
    whole = patches // CHUNK
    main = whole * CHUNK

    me = lax.axis_index("tile")
    core = lax.rem(me, 2)
    ypos = lax.rem(me // 2, 2)
    zpos = me // PLANE
    core_peer = me + 1 - 2 * core
    y_peer = me + 2 - 4 * ypos

    load_w = pltpu.make_async_copy(coeffs, weights, local.at[0])
    load_w.start()
    load_k = pltpu.make_async_copy(
        kinds_all.at[:, pl.ds(pl.multiple_of(me * points, LANES), points)], kinds, local.at[1]
    )
    load_k.start()

    def columns(dst):
        return cot.at[:, pl.ds(pl.multiple_of(dst * points, LANES), points)]

    own = pltpu.make_async_copy(columns(me), recv.at[me], local.at[2])
    own.start()

    barrier = pltpu.get_barrier_semaphore()

    def greet(d, carry):
        pl.semaphore_signal(
            barrier, inc=1, device_id={"tile": lax.rem(me + d, n)}, device_id_type=MESH
        )
        return carry

    lax.fori_loop(1, n, greet, 0)
    pl.semaphore_wait(barrier, n - 1)

    def block_copy(src, dst):
        return pltpu.make_async_remote_copy(
            src_ref=columns(dst),
            dst_ref=recv.at[src],
            send_sem=a_send.at[dst],
            recv_sem=a_recv.at[src],
            device_id={"tile": dst},
            device_id_type=MESH,
        )

    offsets = [n // 2]
    for step in range(1, n // 2):
        offsets += [n // 2 - step, n // 2 + step]
    for d in offsets:
        block_copy(me, lax.rem(me + d, n)).start()

    load_k.wait()
    kind = jnp.broadcast_to(kinds[...], (8, points))
    for k in range(span):
        row = jnp.zeros((8, points), jnp.float32)
        for c in range(types):
            live = jnp.where(k < tap_count[c], ctf[c, k], jnp.float32(0.0))
            row = jnp.where(kind == c, live, row)
        taps[k] = row

    for d in range(1, n):
        block_copy(lax.rem(me + d, n), me).wait_recv()
    own.wait()
    load_w.wait()

    def core_copy(i):
        return pltpu.make_async_remote_copy(
            src_ref=csend.at[i], dst_ref=crecv.at[i], send_sem=c_send.at[i],
            recv_sem=c_recv.at[i], device_id={"tile": core_peer}, device_id_type=MESH,
        )

    def y_copy(i):
        return pltpu.make_async_remote_copy(
            src_ref=ysend.at[i], dst_ref=yrecv.at[i], send_sem=y_send.at[i],
            recv_sem=y_recv.at[i], device_id={"tile": y_peer}, device_id_type=MESH,
        )

    def z_copy(src, dst):
        return pltpu.make_async_remote_copy(
            src_ref=zsend.at[dst], dst_ref=zrecv.at[src], send_sem=z_send.at[dst],
            recv_sem=z_recv.at[src], device_id={"tile": dst * PLANE + lax.rem(me, PLANE)},
            device_id_type=MESH,
        )

    def group_at(i):
        return lax.rem(zpos + 1 + i, groups)

    def compute(i):
        g = group_at(i)
        slot = i % 2

        def fir(ct, carry):
            cols = pl.ds(pl.multiple_of(ct * LANES, LANES), LANES)
            for b in range(PLANE):
                ext[pl.ds(b * hours, hours), :] = recv[g * PLANE + b, :, cols].astype(jnp.float32)
            after = recv[lax.rem(g * PLANE + PLANE, n), :, cols].astype(jnp.float32)
            ext[pl.ds(rows, hours), :] = jnp.where(g < groups - 1, after, jnp.zeros_like(after))
            acc = [jnp.zeros((8, LANES), jnp.float32) for _ in range(rows // 8)]
            for k in range(span):
                tap = taps[k, :, cols]
                for r in range(rows // 8):
                    acc[r] = acc[r] + tap * ext[pl.ds(r * 8 + k, 8), :]
            surf[:, cols] = jnp.concatenate(acc, 0).astype(jnp.bfloat16)
            return carry

        lax.fori_loop(0, tiles, fir, 0)

        def emit(value, cols):
            for y in range(2):
                first = value[(2 * y) * hours:(2 * y + 1) * hours]
                second = value[(2 * y + 1) * hours:(2 * y + 2) * hours]
                csend[i, y, :, cols] = jnp.where(core == 0, second, first).astype(jnp.bfloat16)
                keep[slot, y, :, cols] = jnp.where(core == 0, first, second)

        def mm(j, carry):
            at = pl.ds(pl.multiple_of(j * CHUNK, CHUNK), CHUNK)
            emit(
                lax.dot_general(
                    surf[...], weights[at, :], (((1,), (1,)), ((), ())),
                    preferred_element_type=jnp.float32,
                ),
                at,
            )
            return carry

        lax.fori_loop(0, whole, mm, 0)
        rest = patches - main
        if rest:
            last = lax.dot_general(
                surf[...], weights[pl.ds(main, rest), :], (((1,), (1,)), ((), ())),
                preferred_element_type=jnp.float32,
            ) if rest > 1 else jnp.sum(
                surf[...].astype(jnp.float32) * weights[pl.ds(main, 1), :].astype(jnp.float32),
                axis=1, keepdims=True,
            )
            width = keep.shape[-1] - main
            if width != rest:
                last = jnp.where(
                    lax.broadcasted_iota(jnp.int32, (rows, width), 1) < rest,
                    jnp.broadcast_to(last, (rows, width)),
                    jnp.float32(0.0),
                )
            emit(last, pl.ds(main, width))
        core_copy(i).start()

    def core_done(i):
        slot = i % 2
        core_copy(i).wait_recv()
        ysend[i] = (keep[slot, 1 - ypos] + crecv[i, 1 - ypos].astype(jnp.float32)).astype(
            jnp.bfloat16
        )
        y_copy(i).start()
        ykeep[slot] = keep[slot, ypos] + crecv[i, ypos].astype(jnp.float32)

    def y_done(i):
        slot = i % 2
        y_copy(i).wait_recv()
        value = ykeep[slot] + yrecv[i].astype(jnp.float32)
        if i < groups - 1:
            g = group_at(i)
            zsend[g] = value.astype(jnp.bfloat16)
            z_copy(zpos, g).start()
        else:
            ykeep[slot] = value

    for i in range(groups + 2):
        if i < groups:
            compute(i)
        if i >= 2:
            y_done(i - 2)
        if 1 <= i <= groups:
            core_done(i - 1)

    total = ykeep[(groups - 1) % 2]
    for d in range(1, groups):
        src = lax.rem(zpos + d, groups)
        z_copy(src, zpos).wait_recv()
        total = total + zrecv[src].astype(jnp.float32)
    out[...] = total[:, :patches]

    for d in range(1, n):
        block_copy(me, lax.rem(me + d, n)).wait_send()
    for i in range(groups):
        core_copy(i).wait_send()
        y_copy(i).wait_send()
        if i < groups - 1:
            z_copy(zpos, group_at(i)).wait_send()


def per_device(n, cotangent, coeffs, ctf, tap_count, construction):
    hours = cotangent.shape[0]
    patches, points = coeffs.shape
    groups = n // PLANE
    width = -(-patches // LANES) * LANES
    span = ctf.shape[1]
    rows = PLANE * hours
    bf16, f32 = jnp.bfloat16, jnp.float32
    dma = pltpu.SemaphoreType.DMA
    return pl.pallas_call(
        functools.partial(kernel, n),
        out_shape=jax.ShapeDtypeStruct((hours, patches), f32),
        in_specs=[
            pl.BlockSpec(memory_space=pltpu.HBM),
            pl.BlockSpec(memory_space=pltpu.HBM),
            pl.BlockSpec(memory_space=pltpu.HBM),
            pl.BlockSpec(memory_space=pltpu.SMEM),
            pl.BlockSpec(memory_space=pltpu.SMEM),
        ],
        out_specs=pl.BlockSpec(memory_space=pltpu.VMEM),
        scratch_shapes=[
            pltpu.VMEM((n, hours, points), bf16),
            pltpu.VMEM((patches, points), bf16),
            pltpu.VMEM((1, points), jnp.int32),
            pltpu.VMEM((span, 8, points), f32),
            pltpu.VMEM((rows + hours, LANES), f32),
            pltpu.VMEM((rows, points), bf16),
            pltpu.VMEM((groups, 2, hours, width), bf16),
            pltpu.VMEM((groups, 2, hours, width), bf16),
            pltpu.VMEM((2, 2, hours, width), f32),
            pltpu.VMEM((groups, hours, width), bf16),
            pltpu.VMEM((groups, hours, width), bf16),
            pltpu.VMEM((2, hours, width), f32),
            pltpu.VMEM((groups, hours, width), bf16),
            pltpu.VMEM((groups, hours, width), bf16),
            dma((n,)),
            dma((n,)),
            dma((groups,)),
            dma((groups,)),
            dma((groups,)),
            dma((groups,)),
            dma((groups,)),
            dma((groups,)),
            dma((3,)),
        ],
        compiler_params=pltpu.CompilerParams(
            collective_id=0, has_side_effects=True, vmem_limit_bytes=56 * 2**20
        ),
        name="sky_adjoint",
    )(cotangent, coeffs, construction.reshape(1, -1), ctf, tap_count)


def solution(mesh):
    return jax.shard_map(
        functools.partial(per_device, mesh.shape["tile"]),
        mesh=mesh,
        in_specs=(P("tile", "district"), P(None, ("district", "tile")), P(), P(), P("district")),
        out_specs=P("tile", "district"),
        check_vma=False,
    )
```

time: 149 us -> 63.7 us (0.43)
  waiting for transfers between devices: 68.6 us -> 0 us
  Pallas kernels: 0 us -> 61.9 us
  blocking collectives: 48.2 us -> 0 us
  between operations: 13.5 us -> 0.01 us
  other arithmetic: 7.44 us -> 0 us
  matrix products: 7.16 us -> 0 us
    unnamed x2 -> x0, waiting for transfers between devices: 68.6 us -> none
    pallas_call x0 -> x1, Pallas kernels: none -> 61.9 us  [per_device(): pl.pallas_call(functools.partial(kernel, n), out_shape=jax.ShapeDtypeStru...]
    all_to_all x1 -> x0, blocking collectives: 48.2 us -> none  [per_device(): lax.all_to_all(surface, 'tile', split_axis=1, concat_axis=0, tiled=True)]
    convert_element_type x1 -> x0, other arithmetic: 7.44 us -> none  [correlate(): return accum.astype(jnp.bfloat16)]
    dot_general x2 -> x0, matrix products: 7.16 us -> none  [the longest x1 5.05 us: per_device(): lax.dot_general(by_points, coeffs, (((1,), (1,)), ((), ())), preferred_el...]
    slice x2 -> x0, local copies, waits for them, and re-layouts: 1.98 us -> none  [correlate(): taps[shift_k][None, :]]
    unnamed x7 -> x1, local copies, waits for them, and re-layouts: 0.1 us -> 1.64 us
  transfers between devices with their start and end apart: 2 -> 0, of which waited for: 1 -> 0; matrix products, arithmetic and copies ran while one was open for 3% -> 0% of each run, Pallas kernels for 0% -> 0%
where the time goes in v1:
time: 63.7 us; the launch traced here: 63.5 us
  Pallas kernels  61.9 us (97%)
  local copies, waits for them, and re-layouts  1.64 us (3%)
    pallas_call x1, Pallas kernels, per_device(): pl.pallas_call(functools.partial(kernel, n), out_shape=jax.ShapeDtypeStru...  61.9 us
    unnamed x1, local copies, waits for them, and re-layouts  1.64 us

profile of v1, /device:TPU:0, one launch (start us, length us, event | category | flops | bytes accessed | tf_op | source)
XLA Modules:
  0.0 63.5 jit_solution(1730415168961952640)
XLA Ops:
  0.0 61.9 %sky_adjoint.1 = f32[24,2305]{1,0:T(8,128)} custom-call(bf16[24,24576]{1,0:T(8,128)(2,1)} %cot.1, bf16[2305,1536]{1,0:T(8,128)(2,1)} %coeffs.1, s32[1,24576]{1,0:T(1,128)} %bitcast.1, f32[8,24]{1,0:T(8,128)} %ctf.1, s32[8]{0:T(128)} %tap_count.1), custom_call_target="tpu_custom_call" | custom-call | tf_op jit(solution)/shard_map/sky_adjoint/pallas_call | solution.py:226
  61.9 1.6 %copy.7 = f32[24,2305]{1,0:T(8,128)} copy(f32[24,2305]{1,0:T(8,128)} %sky_adjoint.1) | data formatting | bytes 442560

commit v2 on v1

--- a/solution.py
+++ b/solution.py
@@ -9,8 +9,9 @@
 
 MESH = pl.DeviceIdType.MESH
 LANES = 128
-CHUNK = 256
+CHUNK = 768
 PLANE = 4
+UNITS = 3
 
 
 def kernel(
@@ -90,32 +91,36 @@
     own.wait()
     load_w.wait()
 
-    def core_copy(i):
+    width = keep.shape[-1]
+    units = UNITS if whole % UNITS == 0 else 1
+    step = main // units
+    block = 4 if groups % 4 == 0 else 1
+
+    def span_of(u):
+        return pl.ds(u * step, step if u < units - 1 else width - u * step)
+
+    def core_copy(u):
         return pltpu.make_async_remote_copy(
-            src_ref=csend.at[i], dst_ref=crecv.at[i], send_sem=c_send.at[i],
-            recv_sem=c_recv.at[i], device_id={"tile": core_peer}, device_id_type=MESH,
-        )
-
-    def y_copy(i):
+            src_ref=csend.at[:, :, :, span_of(u)], dst_ref=crecv.at[:, :, :, span_of(u)],
+            send_sem=c_send.at[u], recv_sem=c_recv.at[u],
+            device_id={"tile": core_peer}, device_id_type=MESH,
+        )
+
+    def y_copy(u):
         return pltpu.make_async_remote_copy(
-            src_ref=ysend.at[i], dst_ref=yrecv.at[i], send_sem=y_send.at[i],
-            recv_sem=y_recv.at[i], device_id={"tile": y_peer}, device_id_type=MESH,
-        )
-
-    def z_copy(src, dst):
+            src_ref=ysend.at[:, :, span_of(u)], dst_ref=yrecv.at[:, :, span_of(u)],
+            send_sem=y_send.at[u], recv_sem=y_recv.at[u],
+            device_id={"tile": y_peer}, device_id_type=MESH,
+        )
+
+    def z_copy(src, dst, u):
         return pltpu.make_async_remote_copy(
-            src_ref=zsend.at[dst], dst_ref=zrecv.at[src], send_sem=z_send.at[dst],
-            recv_sem=z_recv.at[src], device_id={"tile": dst * PLANE + lax.rem(me, PLANE)},
-            device_id_type=MESH,
-        )
-
-    def group_at(i):
-        return lax.rem(zpos + 1 + i, groups)
-
-    def compute(i):
-        g = group_at(i)
-        slot = i % 2
-
+            src_ref=zsend.at[dst, :, span_of(u)], dst_ref=zrecv.at[src, :, span_of(u)],
+            send_sem=z_send.at[dst, u], recv_sem=z_recv.at[src, u],
+            device_id={"tile": dst * PLANE + lax.rem(me, PLANE)}, device_id_type=MESH,
+        )
+
+    def fir_group(g, carry):
         def fir(ct, carry):
             cols = pl.ds(pl.multiple_of(ct * LANES, LANES), LANES)
             for b in range(PLANE):
@@ -127,91 +132,119 @@
                 tap = taps[k, :, cols]
                 for r in range(rows // 8):
                     acc[r] = acc[r] + tap * ext[pl.ds(r * 8 + k, 8), :]
-            surf[:, cols] = jnp.concatenate(acc, 0).astype(jnp.bfloat16)
+            at = pl.ds(pl.multiple_of(g * rows, rows), rows)
+            surf[at, cols] = jnp.concatenate(acc, 0).astype(jnp.bfloat16)
             return carry
 
         lax.fori_loop(0, tiles, fir, 0)
-
-        def emit(value, cols):
+        return carry
+
+    lax.fori_loop(0, groups, fir_group, 0)
+
+    def emit(value, mb, cols):
+        for q in range(block):
             for y in range(2):
-                first = value[(2 * y) * hours:(2 * y + 1) * hours]
-                second = value[(2 * y + 1) * hours:(2 * y + 2) * hours]
-                csend[i, y, :, cols] = jnp.where(core == 0, second, first).astype(jnp.bfloat16)
-                keep[slot, y, :, cols] = jnp.where(core == 0, first, second)
-
+                top = (PLANE * q + 2 * y) * hours
+                first = value[top:top + hours]
+                second = value[top + hours:top + 2 * hours]
+                g = mb * block + q
+                csend[g, y, :, cols] = jnp.where(core == 0, second, first).astype(jnp.bfloat16)
+                keep[g, y, :, cols] = jnp.where(core == 0, first, second)
+
+    def band(mb):
+        return surf[pl.ds(pl.multiple_of(mb * block * rows, block * rows), block * rows), :]
+
+    def compute(u):
         def mm(j, carry):
             at = pl.ds(pl.multiple_of(j * CHUNK, CHUNK), CHUNK)
-            emit(
-                lax.dot_general(
-                    surf[...], weights[at, :], (((1,), (1,)), ((), ())),
-                    preferred_element_type=jnp.float32,
-                ),
-                at,
-            )
-            return carry
-
-        lax.fori_loop(0, whole, mm, 0)
-        rest = patches - main
-        if rest:
-            last = lax.dot_general(
-                surf[...], weights[pl.ds(main, rest), :], (((1,), (1,)), ((), ())),
-                preferred_element_type=jnp.float32,
-            ) if rest > 1 else jnp.sum(
-                surf[...].astype(jnp.float32) * weights[pl.ds(main, 1), :].astype(jnp.float32),
+
+            def part(mb, carry):
+                emit(
+                    lax.dot_general(
+                        band(mb), weights[at, :], (((1,), (1,)), ((), ())),
+                        preferred_element_type=jnp.float32,
+                    ),
+                    mb, at,
+                )
+                return carry
+
+            return lax.fori_loop(0, groups // block, part, carry)
+
+        lax.fori_loop(u * (whole // units), (u + 1) * (whole // units), mm, 0)
+        core_copy(u).start()
+
+    rest = patches - main
+
+    def edge(mb, carry):
+        if rest == 1:
+            last = jnp.sum(
+                band(mb).astype(jnp.float32) * weights[pl.ds(main, 1), :].astype(jnp.float32),
                 axis=1, keepdims=True,
             )
-            width = keep.shape[-1] - main
-            if width != rest:
-                last = jnp.where(
-                    lax.broadcasted_iota(jnp.int32, (rows, width), 1) < rest,
-                    jnp.broadcast_to(last, (rows, width)),
-                    jnp.float32(0.0),
-                )
-            emit(last, pl.ds(main, width))
-        core_copy(i).start()
-
-    def core_done(i):
-        slot = i % 2
-        core_copy(i).wait_recv()
-        ysend[i] = (keep[slot, 1 - ypos] + crecv[i, 1 - ypos].astype(jnp.float32)).astype(
-            jnp.bfloat16
-        )
-        y_copy(i).start()
-        ykeep[slot] = keep[slot, ypos] + crecv[i, ypos].astype(jnp.float32)
-
-    def y_done(i):
-        slot = i % 2
-        y_copy(i).wait_recv()
-        value = ykeep[slot] + yrecv[i].astype(jnp.float32)
-        if i < groups - 1:
-            g = group_at(i)
-            zsend[g] = value.astype(jnp.bfloat16)
-            z_copy(zpos, g).start()
         else:
-            ykeep[slot] = value
-
-    for i in range(groups + 2):
-        if i < groups:
-            compute(i)
-        if i >= 2:
-            y_done(i - 2)
-        if 1 <= i <= groups:
-            core_done(i - 1)
-
-    total = ykeep[(groups - 1) % 2]
-    for d in range(1, groups):
-        src = lax.rem(zpos + d, groups)
-        z_copy(src, zpos).wait_recv()
-        total = total + zrecv[src].astype(jnp.float32)
-    out[...] = total[:, :patches]
+            last = lax.dot_general(
+                band(mb), weights[pl.ds(main, rest), :], (((1,), (1,)), ((), ())),
+                preferred_element_type=jnp.float32,
+            )
+        shape = (block * rows, width - main)
+        if width - main != rest:
+            last = jnp.where(
+                lax.broadcasted_iota(jnp.int32, shape, 1) < rest,
+                jnp.broadcast_to(last, shape),
+                jnp.float32(0.0),
+            )
+        emit(last, mb, pl.ds(main, width - main))
+        return carry
+
+    if rest:
+        lax.fori_loop(0, groups // block, edge, 0)
+
+    def core_done(u):
+        cols = span_of(u)
+        core_copy(u).wait_recv()
+        for g in range(groups):
+            ysend[g, :, cols] = (
+                keep[g, 1 - ypos, :, cols] + crecv[g, 1 - ypos, :, cols].astype(jnp.float32)
+            ).astype(jnp.bfloat16)
+        y_copy(u).start()
+        for g in range(groups):
+            ykeep[g, :, cols] = keep[g, ypos, :, cols] + crecv[g, ypos, :, cols].astype(jnp.float32)
+
+    def y_done(u):
+        cols = span_of(u)
+        y_copy(u).wait_recv()
+        for d in range(1, groups):
+            g = lax.rem(zpos + d, groups)
+            zsend[g, :, cols] = (
+                ykeep[g, :, cols] + yrecv[g, :, cols].astype(jnp.float32)
+            ).astype(jnp.bfloat16)
+            z_copy(zpos, g, u).start()
+
+    for u in range(units + 2):
+        if u < units:
+            compute(u)
+        if 1 <= u <= units:
+            core_done(u - 1)
+        if u >= 2:
+            y_done(u - 2)
+
+    for u in range(units):
+        cols = span_of(u)
+        total = ykeep[zpos, :, cols] + yrecv[zpos, :, cols].astype(jnp.float32)
+        for d in range(1, groups):
+            src = lax.rem(zpos + d, groups)
+            z_copy(src, zpos, u).wait_recv()
+            total = total + zrecv[src, :, cols].astype(jnp.float32)
+        size = step if u < units - 1 else patches - u * step
+        out[:, pl.ds(u * step, size)] = total[:, :size]
 
     for d in range(1, n):
         block_copy(me, lax.rem(me + d, n)).wait_send()
-    for i in range(groups):
-        core_copy(i).wait_send()
-        y_copy(i).wait_send()
-        if i < groups - 1:
-            z_copy(zpos, group_at(i)).wait_send()
+    for u in range(units):
+        core_copy(u).wait_send()
+        y_copy(u).wait_send()
+        for d in range(1, groups):
+            z_copy(zpos, lax.rem(zpos + d, groups), u).wait_send()
 
 
 def per_device(n, cotangent, coeffs, ctf, tap_count, construction):
@@ -240,23 +273,23 @@
             pltpu.VMEM((1, points), jnp.int32),
             pltpu.VMEM((span, 8, points), f32),
             pltpu.VMEM((rows + hours, LANES), f32),
-            pltpu.VMEM((rows, points), bf16),
+            pltpu.VMEM((groups * rows, points), bf16),
             pltpu.VMEM((groups, 2, hours, width), bf16),
             pltpu.VMEM((groups, 2, hours, width), bf16),
-            pltpu.VMEM((2, 2, hours, width), f32),
+            pltpu.VMEM((groups, 2, hours, width), f32),
             pltpu.VMEM((groups, hours, width), bf16),
             pltpu.VMEM((groups, hours, width), bf16),
-            pltpu.VMEM((2, hours, width), f32),
+            pltpu.VMEM((groups, hours, width), f32),
             pltpu.VMEM((groups, hours, width), bf16),
             pltpu.VMEM((groups, hours, width), bf16),
             dma((n,)),
             dma((n,)),
-            dma((groups,)),
-            dma((groups,)),
-            dma((groups,)),
-            dma((groups,)),
-            dma((groups,)),
-            dma((groups,)),
+            dma((UNITS,)),
+            dma((UNITS,)),
+            dma((UNITS,)),
+            dma((UNITS,)),
+            dma((groups, UNITS)),
+            dma((groups, UNITS)),
             dma((3,)),
         ],
         compiler_params=pltpu.CompilerParams(

time: 63.7 us -> 60.1 us (0.943)
  Pallas kernels: 61.9 us -> 58.2 us
    pallas_call x1, Pallas kernels: 61.9 us -> 58.2 us  [per_device(): pl.pallas_call(functools.partial(kernel, n), out_shape=jax.ShapeDtypeStru...]
where the time goes in v2:
time: 60.1 us; the launch traced here: 59.9 us
  Pallas kernels  58.2 us (97%)
  local copies, waits for them, and re-layouts  1.64 us (3%)
    pallas_call x1, Pallas kernels, per_device(): pl.pallas_call(functools.partial(kernel, n), out_shape=jax.ShapeDtypeStru...  58.2 us
    unnamed x1, local copies, waits for them, and re-layouts  1.64 us

profile of v2, /device:TPU:0, one launch (start us, length us, event | category | flops | bytes accessed | tf_op | source)
XLA Modules:
  0.0 59.9 jit_solution(7271004163648914752)
XLA Ops:
  0.0 58.2 %sky_adjoint.1 = f32[24,2305]{1,0:T(8,128)} custom-call(bf16[24,24576]{1,0:T(8,128)(2,1)} %cot.1, bf16[2305,1536]{1,0:T(8,128)(2,1)} %coeffs.1, s32[1,24576]{1,0:T(1,128)} %bitcast.1, f32[8,24]{1,0:T(8,128)} %ctf.1, s32[8]{0:T(128)} %tap_count.1), custom_call_target="tpu_custom_call" | custom-call | tf_op jit(solution)/shard_map/sky_adjoint/pallas_call | solution.py:259
  58.2 1.6 %copy.7 = f32[24,2305]{1,0:T(8,128)} copy(f32[24,2305]{1,0:T(8,128)} %sky_adjoint.1) | data formatting | bytes 442560

commit v3 on v2

--- a/solution.py
+++ b/solution.py
@@ -86,10 +86,27 @@
             row = jnp.where(kind == c, live, row)
         taps[k] = row
 
-    for d in range(1, n):
-        block_copy(lax.rem(me + d, n), me).wait_recv()
     own.wait()
-    load_w.wait()
+    low = zpos < groups // 2
+
+    def arrive(b):
+        @pl.when(me != b)
+        def _():
+            block_copy(b, me).wait_recv()
+
+    def arrive_group(i):
+        @pl.when(low)
+        def _():
+            if i == 0:
+                arrive(0)
+            for b in range(PLANE * i + 1, min(PLANE * (i + 1) + 1, n)):
+                arrive(b)
+
+        @pl.when(jnp.logical_not(low))
+        def _():
+            for b in range(PLANE * (groups - 1 - i), PLANE * (groups - i)):
+                arrive(b)
+
 
     width = keep.shape[-1]
     units = UNITS if whole % UNITS == 0 else 1
@@ -125,7 +142,7 @@
             cols = pl.ds(pl.multiple_of(ct * LANES, LANES), LANES)
             for b in range(PLANE):
                 ext[pl.ds(b * hours, hours), :] = recv[g * PLANE + b, :, cols].astype(jnp.float32)
-            after = recv[lax.rem(g * PLANE + PLANE, n), :, cols].astype(jnp.float32)
+            after = recv[jnp.minimum(g * PLANE + PLANE, n - 1), :, cols].astype(jnp.float32)
             ext[pl.ds(rows, hours), :] = jnp.where(g < groups - 1, after, jnp.zeros_like(after))
             acc = [jnp.zeros((8, LANES), jnp.float32) for _ in range(rows // 8)]
             for k in range(span):
@@ -139,7 +156,10 @@
         lax.fori_loop(0, tiles, fir, 0)
         return carry
 
-    lax.fori_loop(0, groups, fir_group, 0)
+    for i in range(groups):
+        arrive_group(i)
+        fir_group(jnp.where(low, i, groups - 1 - i), 0)
+    load_w.wait()
 
     def emit(value, mb, cols):
         for q in range(block):

time: 60.1 us -> 58.2 us (0.968)
  Pallas kernels: 58.2 us -> 56.3 us
    pallas_call x1, Pallas kernels: 58.2 us -> 56.3 us  [per_device(): pl.pallas_call(functools.partial(kernel, n), out_shape=jax.ShapeDtypeStru...]
where the time goes in v3:
time: 58.2 us; the launch traced here: 58 us
  Pallas kernels  56.3 us (97%)
  local copies, waits for them, and re-layouts  1.64 us (3%)
    pallas_call x1, Pallas kernels, per_device(): pl.pallas_call(functools.partial(kernel, n), out_shape=jax.ShapeDtypeStru...  56.3 us
    unnamed x1, local copies, waits for them, and re-layouts  1.64 us

profile of v3, /device:TPU:0, one launch (start us, length us, event | category | flops | bytes accessed | tf_op | source)
XLA Modules:
  0.0 58.0 jit_solution(9254317193782772602)
XLA Ops:
  0.0 56.3 %sky_adjoint.1 = f32[24,2305]{1,0:T(8,128)} custom-call(bf16[24,24576]{1,0:T(8,128)(2,1)} %cot.1, bf16[2305,1536]{1,0:T(8,128)(2,1)} %coeffs.1, s32[1,24576]{1,0:T(1,128)} %bitcast.1, f32[8,24]{1,0:T(8,128)} %ctf.1, s32[8]{0:T(128)} %tap_count.1), custom_call_target="tpu_custom_call" | custom-call | tf_op jit(solution)/shard_map/sky_adjoint/pallas_call | solution.py:279
  56.4 1.6 %copy.7 = f32[24,2305]{1,0:T(8,128)} copy(f32[24,2305]{1,0:T(8,128)} %sky_adjoint.1) | data formatting | bytes 442560
